TPU v7x, 32 devices: a whole 2x2x4 slice. The times are simulated.
32 devices in a mesh: ctx: 16 (over z, y, core), tp: 2 (over x).
Axes of the slice: x: 2, y: 2, z: 4, core: 2. Of those that a mesh axis runs over, the one named last changes fastest.
Arguments:
- tokens: bfloat16 [8192, 5376], P('ctx'), may hold values from -6 to 6
- query_weight: bfloat16 [5376, 2048], P('ctx', 'tp'), may hold values from -0.078125 to 0.078125
- key_matrix: bfloat16 [5376, 1024], P('ctx', 'tp'), may hold values from -0.078125 to 0.078125
- value_matrix: bfloat16 [5376, 1024], P('ctx', 'tp'), may hold values from -0.078125 to 0.078125
- query_gain: float32 [128], replicated, may hold values from 0.5 to 2.5
- key_norm_gain: float32 [128], replicated, may hold values from 0.5 to 2.5
- cotangent: bfloat16 [8192, 2048], P('ctx', 'tp'), may hold values from -24 to 24
Outputs:
- attended: bfloat16 [8192, 2048], P('ctx', 'tp')
- token_gradient: bfloat16 [8192, 5376], P('ctx', 'tp')
- query_gradient: bfloat16 [5376, 2048], P('ctx', 'tp')
- key_weight_gradient: bfloat16 [5376, 1024], P('ctx', 'tp')
- value_weight_gradient: bfloat16 [5376, 1024], P('ctx', 'tp')
All inputs are finite; a program needn't handle non-finite values.
Results may differ from a plain program's by a relative error of at most 0.035.
Values may be sent and summed in bfloat16 or wider, within the bound.
A program may use at most 128 MiB of HBM per device.

v0:
```python
import jax
import jax.numpy as jnp
from jax import lax
from jax.sharding import PartitionSpec as P

HEAD_WIDTH = 128
WINDOW_LENGTH = 1024
QUERY_SCALAR = 168


rope_base = 10000.0
norm_eps = 1e-06


def passed_along(shard, axis, by):
    size = lax.axis_size(axis)
    pairs = [(i, i + by) for i in range(size) if 0 <= i + by < size]
    return lax.ppermute(shard, axis, pairs)


def normalize_and_rotate(unnormed_rows, gain_vector, token_positions, head_count, head_size):
    row_total = unnormed_rows.shape[0]
    shaped = unnormed_rows.reshape(row_total, head_count, head_size)
    mean_square = jnp.mean(shaped * shaped, axis=-1, keepdims=True)
    normed = shaped * lax.rsqrt(mean_square + norm_eps) * gain_vector
    half_size = head_size // 2
    inverse = jnp.power(
        jnp.float32(rope_base), -jnp.arange(0, head_size, 2).astype(jnp.float32) / head_size
    )
    angles = token_positions[:, None] * inverse[None, :]
    cosine = jnp.cos(angles)[:, None, :]
    sine_part = jnp.sin(angles)[:, None, :]
    leading = normed[..., :half_size]
    trailing = normed[..., half_size:]
    turned = jnp.concatenate(
        [leading * cosine - trailing * sine_part, trailing * cosine + leading * sine_part], axis=-1
    )
    return turned.reshape(row_total, head_count * head_size)


def band_attention(
    query_rows, key_row_block, value_row_block, output_rows, first_query, first_key, score_scale
):
    scores = (
        jnp.einsum("tkgd,ckd->kgtc", query_rows, key_row_block, preferred_element_type=jnp.float32)
        * score_scale
    )
    query_place = first_query + jnp.arange(query_rows.shape[0], dtype=jnp.int32)
    key_place = first_key + jnp.arange(key_row_block.shape[0], dtype=jnp.int32)
    visible = (
        (key_place[None, :] >= 0)
        & (key_place[None, :] <= query_place[:, None])
        & (key_place[None, :] > query_place[:, None] - WINDOW_LENGTH)
    )
    exponent_terms = jnp.where(visible, jnp.exp(scores), 0.0)
    totals = jnp.sum(exponent_terms, axis=-1, keepdims=True)
    probs = exponent_terms / totals
    weights = probs.astype(jnp.bfloat16)
    mixed = jnp.einsum(
        "kgtc,ckd->tkgd", weights, value_row_block, preferred_element_type=jnp.float32
    )
    attended = mixed.astype(jnp.bfloat16)
    delta = jnp.sum(
        output_rows.astype(jnp.float32) * lax.optimization_barrier(attended).astype(jnp.float32),
        axis=-1,
    )
    delta = jnp.transpose(delta, (1, 2, 0))[..., None]
    prob_grads = jnp.einsum(
        "tkgd,ckd->kgtc", output_rows, value_row_block, preferred_element_type=jnp.float32
    )
    score_grads = (probs * (prob_grads - delta)).astype(jnp.bfloat16)
    query_grads = (
        jnp.einsum("kgtc,ckd->tkgd", score_grads, key_row_block, preferred_element_type=jnp.float32)
        * score_scale
    )
    key_grads = (
        jnp.einsum("kgtc,tkgd->ckd", score_grads, query_rows, preferred_element_type=jnp.float32)
        * score_scale
    )
    value_grads = jnp.einsum(
        "kgtc,tkgd->ckd", weights, output_rows, preferred_element_type=jnp.float32
    )
    return (attended, query_grads, key_grads, value_grads)


def transposed(left_rows, right_rows):
    return lax.dot_general(
        left_rows, right_rows, (((1,), (1,)), ((), ())), preferred_element_type=jnp.float32
    )


def shards(tokens, query_weight, key_matrix, value_matrix, query_gain, key_norm_gain, cotangent):
    row_count = tokens.shape[0]
    heads_query = query_weight.shape[1] // HEAD_WIDTH
    heads_key = key_matrix.shape[1] // HEAD_WIDTH
    group_width = heads_query // heads_key
    reach_back = WINDOW_LENGTH // row_count
    score_scale = QUERY_SCALAR ** (-0.5)
    first_row = lax.axis_index("ctx") * row_count
    token_positions = (first_row + jnp.arange(row_count, dtype=jnp.int32)).astype(jnp.float32)
    full_query, full_key, full_value = (
        lax.all_gather(query_weight, "ctx", axis=0, tiled=True),
        lax.all_gather(key_matrix, "ctx", axis=0, tiled=True),
        lax.all_gather(value_matrix, "ctx", axis=0, tiled=True),
    )
    query_raw = jnp.dot(tokens, full_query, preferred_element_type=jnp.float32)
    key_raw = jnp.dot(tokens, full_key, preferred_element_type=jnp.float32)
    value_unprojected = jnp.dot(tokens, full_value, preferred_element_type=jnp.float32)

    def rotate_queries(unnormed_rows):
        return normalize_and_rotate(
            unnormed_rows, query_gain, token_positions, heads_query, HEAD_WIDTH
        )

    def rotate_keys(unnormed_rows):
        return normalize_and_rotate(
            unnormed_rows, key_norm_gain, token_positions, heads_key, HEAD_WIDTH
        )

    query_after_rotation, query_pull = jax.vjp(rotate_queries, query_raw)
    key_after_rotation, key_pullback = jax.vjp(rotate_keys, key_raw)
    query_rows = query_after_rotation.astype(jnp.bfloat16).reshape(
        row_count, heads_key, group_width, HEAD_WIDTH
    )
    stacked = jnp.stack(
        [
            key_after_rotation.astype(jnp.bfloat16).reshape(row_count, heads_key, HEAD_WIDTH),
            value_unprojected.astype(jnp.bfloat16).reshape(row_count, heads_key, HEAD_WIDTH),
        ]
    )
    arrivals = []
    carried = stacked
    for hop_count in range(reach_back):
        carried = passed_along(carried, "ctx", 1)
        arrivals.append(carried)
    band_rows = jnp.concatenate(arrivals[::-1] + [stacked], axis=1)
    output_rows = cotangent.reshape(row_count, heads_key, group_width, HEAD_WIDTH)
    attended, query_grads, key_grads, value_grads = band_attention(
        query_rows,
        band_rows[0],
        band_rows[1],
        output_rows,
        first_row,
        first_row - WINDOW_LENGTH,
        score_scale,
    )
    band_grads = jnp.stack([key_grads, value_grads])

    def band_tile(distance):
        lowest = (reach_back - distance) * row_count
        return band_grads[:, lowest : lowest + row_count]

    returned = band_tile(reach_back)
    for hop_count in range(1, reach_back + 1):
        returned = passed_along(returned.astype(jnp.bfloat16), "ctx", -1).astype(
            returned.dtype
        ) + band_tile(reach_back - hop_count)
    (query_back,) = query_pull(query_grads.reshape(row_count, heads_query * HEAD_WIDTH))
    (key_backprop,) = key_pullback(returned[0].reshape(row_count, heads_key * HEAD_WIDTH))
    query_back = query_back.astype(jnp.bfloat16)
    key_backprop = key_backprop.astype(jnp.bfloat16)
    value_backprop = returned[1].reshape(row_count, heads_key * HEAD_WIDTH).astype(jnp.bfloat16)
    token_terms = (
        transposed(query_back, full_query)
        + transposed(key_backprop, full_key)
        + transposed(value_backprop, full_value)
    )
    token_gradient = lax.psum_scatter(
        token_terms.astype(jnp.bfloat16), "tp", scatter_dimension=1, tiled=True
    )

    def reduce_rows(grad_rows):
        return lax.psum_scatter(
            lax.dot_general(
                tokens, grad_rows, (((0,), (0,)), ((), ())), preferred_element_type=jnp.float32
            ).astype(jnp.bfloat16),
            "ctx",
            scatter_dimension=0,
            tiled=True,
        )

    query_gradient = reduce_rows(query_back)
    pair_gradient = reduce_rows(jnp.concatenate([key_backprop, value_backprop], axis=1))
    key_columns = key_matrix.shape[1]
    return (
        attended.reshape(row_count, heads_query * HEAD_WIDTH),
        token_gradient,
        query_gradient,
        pair_gradient[:, :key_columns],
        pair_gradient[:, key_columns:],
    )


def solution(mesh):
    in_specs = (
        P("ctx", None),
        P("ctx", "tp"),
        P("ctx", "tp"),
        P("ctx", "tp"),
        P(),
        P(),
        P("ctx", "tp"),
    )
    out_specs = (P("ctx", "tp"), P("ctx", "tp"), P("ctx", "tp"), P("ctx", "tp"), P("ctx", "tp"))
    return jax.shard_map(shards, mesh=mesh, in_specs=in_specs, out_specs=out_specs, check_vma=False)
```

profile of v0, /device:TPU:0, one launch (start us, length us, event | category | flops | bytes accessed | tf_op | source)
XLA Modules:
  0.0 725.7 jit_solution(8253878694538589952)
XLA Ops:
  10.4 60.0 %all-gather.6.cloned.1.call-done = bf16[5376,512]{1,0:T(8,128)(2,1)} async-done(((bf16[336,512]{1,0:T(8,128)(2,1)}), bf16[5376,512]{1,0:T(8,128)(2,1)}) %all-gather.6.cloned.1.call-update) | async-done | bytes 5505040 | tf_op jit(solution)/shard_map/all_gather | solution.py:104
  70.4 7.2 convolution_convert_fusion.2
  77.9 50.8 %all-gather.4.cloned.1.call-done = bf16[5376,512]{1,0:T(8,128)(2,1)} async-done(((bf16[336,512]{1,0:T(8,128)(2,1)}), bf16[5376,512]{1,0:T(8,128)(2,1)}) %all-gather.4.cloned.1.call-update) | async-done | bytes 5505040 | tf_op jit(solution)/shard_map/all_gather | solution.py:103
  128.7 6.7 multiply_reduce_fusion.4
  137.3 3.2 collective-permute-start
  140.5 1.4 collective-permute-done
  141.9 17.3 %collective-permute-start.1 = (bf16[2,512,4,128]{3,1,2,0:T(8,128)(2,1)}, bf16[2,512,4,128]{3,1,2,0:T(8,128)(2,1)S(1)}, u32[]{:S(2)}, u32[]{:S(2)}) collective-permute-start(bf16[2,512,4,128]{3,1,2,0:T(8,128)(2,1)} %collective-permute-done), channel_id=1, source_target_pairs={{0,2},{2,4},{4,6},{6,8},{8,10},{10,12},{12,14},{14,16},{16,18},{18... | collective-permute-start | bytes 3145736 | tf_op jit(solution)/shard_map/ppermute | solution.py:18
  159.2 2.3 copy.115
  161.5 1.9 compare_and_fusion
  163.5 3.1 maximum_maximum_fusion
  166.6 71.6 %all-gather.8.cloned.1.call-done = bf16[5376,1024]{1,0:T(8,128)(2,1)} async-done(((bf16[336,1024]{1,0:T(8,128)(2,1)}), bf16[5376,1024]{1,0:T(8,128)(2,1)}) %all-gather.8.cloned.1.call-update) | async-done | bytes 11010064 | tf_op jit(solution)/shard_map/all_gather | solution.py:102
  238.2 10.2 %convolution_bitcast_fusion.1 = f32[64,8,8,128]{3,1,2,0:T(8,128)S(1)} fusion(bf16[512,5376]{1,0:T(8,128)(2,1)} %param.7, bf16[5376,1024]{1,0:T(8,128)(2,1)} %all-gather.8.cloned.1.call-done), kind=kOutput, calls=%fused_computation.44 | convolution fusion | flops 5637144576 | bytes 18612224 | tf_op jit(solution)/shard_map/dot_general | solution.py:106
  252.3 1.5 copy-done.7
  254.0 11.4 %fusion.3 = (f32[4,2,512]{2,1,0:T(2,128)S(1)}, f32[4,1536,512,2]{2,1,3,0:T(8,128)}) fusion(pred[512,1536]{0,1:T(8,128)(4,1)S(1)} %copy-done.15, bf16[512,4,2,128]{3,0,2,1:T(8,128)(2,1)S(1)} %bitcast.125, bf16[2,1536,4,128]{3,1,2,0:T(8,128)(2,1)S(1)} %copy-done.7), kind=kOutput, calls=%fused_computation.5 | convolution fusion | flops 1629483008 | bytes 28590080 | tf_op jit(solution)/shard_map/tkgd,ckd->kgtc/dot_general | solution.py:45
  265.3 11.6 %fusion.22 = bf16[4,128,2,512]{3,1,2,0:T(8,128)(2,1)S(1)} fusion(bf16[2,1536,4,128]{3,1,2,0:T(8,128)(2,1)S(1)} %copy-done.7, f32[4,1536,512,2]{2,1,3,0:T(8,128)} %get-tuple-element.47, f32[4,2,512]{2,1,0:T(2,128)S(1)} %get-tuple-element.46, pred[512,1536]{0,1:T(8,128)(4,1)S(1)} %copy-done.15), kind=kOutput, calls=%fused_computation.48 | convolution fusion | flops 1636302848 | bytes 28590080 | tf_op jit(solution)/shard_map/kgtc,ckd->tkgd/dot_general | solution.py:59
  277.3 12.3 %fusion.10 = f32[1,1536,4,128]{3,1,2,0:T(8,128)} fusion(bf16[512,4,2,128]{0,3,2,1:T(8,128)(2,1)S(1)} %bitcast.130, f32[4,1536,512,2]{2,1,3,0:T(8,128)} %get-tuple-element.47, f32[4,2,512]{2,1,0:T(2,128)S(1)} %get-tuple-element.46, pred[512,1536]{0,1:T(8,128)(4,1)S(1)} %copy-done.15), kind=kOutput, calls=%fused_computation.20 | convolution fusion | flops 1635778560 | bytes 30162944 | tf_op jit(solution)/shard_map/kgtc,tkgd->ckd/dot_general | solution.py:80
  289.6 16.0 %fusion.1 = bf16[4,2,512,1536]{2,3,1,0:T(8,128)(2,1)} fusion(bf16[512,4,2,128]{0,3,2,1:T(8,128)(2,1)} %bitcast.129, f32[4,2,512]{2,1,0:T(2,128)S(1)} %bitcast.140, bf16[2,1536,4,128]{3,1,2,0:T(8,128)(2,1)} %maximum_maximum_fusion, f32[4,2,512]{2,1,0:T(2,128)S(1)} %get-tuple-element.46, f32[4,1536,512,2]{2,1,3,0:T(8,128)} %get-tuple-element.47, ...), kind=kOutput, calls=%fused_computation.2 | convolution fusion | flops 1648361472 | bytes 41189376 | tf_op jit(solution)/shard_map/tkgd,ckd->kgtc/dot_general | solution.py:68
  305.6 7.1 convolution_multiply_fusion
  312.8 1.5 copy-done.1
  314.5 5.2 fusion.14
  319.7 1.5 fusion.44
  321.2 3.2 copy.162
  324.4 2.7 fusion.20
  327.1 1.3 collective-permute-start.2
  328.4 3.2 copy.163
  331.6 2.7 multiply_add_fusion.1
  334.3 1.3 copy-done.3
  336.3 1.2 multiply_reduce_fusion
  337.8 4.6 fusion.15
  342.4 1.8 fusion.18
  344.3 1.3 collective-permute-start.3
  345.6 12.9 %fusion.28 = f32[512,5376]{1,0:T(8,128)} fusion(bf16[5376,1024]{1,0:T(8,128)(2,1)} %all-gather.8.cloned.1.call-done, bf16[64,8,8,128]{3,2,1,0:T(8,128)(2,1)S(1)} %bitcast.136), kind=kOutput, calls=%fused_computation.53 | convolution fusion | flops 5637144576 | bytes 23068672 | tf_op jit(solution)/shard_map/dot_general | solution.py:87
  359.7 1.3 copy.131
  363.4 8.3 %fusion.46 = f32[512,5376]{1,0:T(8,128)} fusion(bf16[512,512]{0,1:T(8,128)(2,1)S(1)} %bitcast.134, bf16[5376,512]{1,0:T(8,128)(2,1)} %all-gather.4.cloned.1.call-done), kind=kOutput, calls=%fused_computation.91 | convolution fusion | flops 2818572288 | bytes 17039360 | tf_op jit(solution)/shard_map/dot_general | solution.py:87
  371.7 13.3 %add_convert_fusion = bf16[512,5376]{1,0:T(8,128)(2,1)} fusion(f32[512,5376]{1,0:T(8,128)} %fusion.28, f32[512,5376]{1,0:T(8,128)} %fusion.46, bf16[512,512]{0,1:T(8,128)(2,1)S(1)} %bitcast.132, bf16[5376,512]{1,0:T(8,128)(2,1)} %all-gather.6.cloned.1.call-done), kind=kOutput, calls=%fused_computation.8 | convolution fusion | flops 2826829824 | bytes 33554432 | tf_op jit(solution)/shard_map/dot_general | solution.py:87
  385.0 8.3 %copy.156 = bf16[512,5376]{0,1:T(8,128)(2,1)} copy(bf16[512,5376]{1,0:T(8,128)(2,1)} %add_convert_fusion) | data formatting | bytes 11010048
  393.4 11.7 %fusion.5 = bf16[5376,1024]{0,1:T(8,128)(2,1)} fusion(bf16[512,5376]{1,0:T(8,128)(2,1)} %param.7, bf16[512,512]{0,1:T(8,128)(2,1)S(1)} %bitcast.133, bf16[512,512]{0,1:T(8,128)(2,1)S(1)} %bitcast.135), kind=kOutput, calls=%fused_computation.10 | convolution fusion | flops 5644746752 | bytes 17563648 | tf_op jit(solution)/shard_map/dot_general | solution.py:174
  405.1 14.7 %copy.160 = bf16[5376,1024]{1,0:T(8,128)(2,1)} copy(bf16[5376,1024]{0,1:T(8,128)(2,1)} %fusion.5) | data formatting | bytes 22020096
  419.9 1.3 copy-done.14
  421.1 11.3 %fusion.4 = bf16[5376,1024]{0,1:T(8,128)(2,1)} fusion(bf16[512,5376]{1,0:T(8,128)(2,1)} %param.7, bf16[64,8,8,128]{3,2,1,0:T(8,128)(2,1)S(1)} %bitcast.137), kind=kOutput, calls=%fused_computation.9 | convolution fusion | flops 5642649600 | bytes 17563648 | tf_op jit(solution)/shard_map/dot_general | solution.py:174
  432.4 14.7 %copy.158 = bf16[5376,1024]{1,0:T(8,128)(2,1)} copy(bf16[5376,1024]{0,1:T(8,128)(2,1)} %fusion.4) | data formatting | bytes 22020096
  447.2 1.2 copy-done.11
  448.4 1.3 copy.132
  449.7 14.6 %reduce-scatter.10.cloned.1.call-done = bf16[2688,512]{1,0:T(8,128)(2,1)} async-done(((bf16[5376,512]{1,0:T(8,128)(2,1)}), bf16[2688,512]{1,0:T(8,128)(2,1)}) %reduce-scatter.10.cloned.1.call-update) | async-done | bytes 2752528
  464.3 4.5 copy.157
  468.8 122.7 %reduce-scatter.14.cloned.1.call-done = bf16[336,1024]{1,0:T(8,128)(2,1)} async-done(((bf16[5376,1024]{1,0:T(8,128)(2,1)}), bf16[336,1024]{1,0:T(8,128)(2,1)}) %reduce-scatter.14.cloned.1.call-update) | async-done | bytes 688144
  591.5 2.0 fusion.45
  593.5 125.1 %reduce-scatter.12.cloned.1.call-done = bf16[336,1024]{1,0:T(8,128)(2,1)} async-done(((bf16[5376,1024]{1,0:T(8,128)(2,1)}), bf16[336,1024]{1,0:T(8,128)(2,1)}) %reduce-scatter.12.cloned.1.call-update) | async-done | bytes 688144
  (89 shorter events, 14.3 us)
Async XLA Ops:
  7.2 63.2 %all-gather.6.cloned.1.call-start = ((), (), s32[]{:S(2)}) async-start(), calls=%async_computation.4 | async-start | bytes 5849088 | tf_op jit(solution)/shard_map/all_gather | solution.py:104
  7.9 120.8 %all-gather.4.cloned.1.call-start = ((), (), s32[]{:S(2)}) async-start(), calls=%async_computation.3 | async-start | bytes 5849088 | tf_op jit(solution)/shard_map/all_gather | solution.py:103
  8.6 229.5 %all-gather.8.cloned.1.call-start = ((), (), s32[]{:S(2)}) async-start(), calls=%async_computation.5 | async-start | bytes 11698176 | tf_op jit(solution)/shard_map/all_gather | solution.py:102
  9.4 454.9 %reduce-scatter.10.cloned.1.call-start = ((), (), s32[]{:S(2)}) async-start(), calls=%async_computation.6 | async-start | bytes 8257536
  77.9 57.9 %copy-start.21 = (f32[128]{0:T(128)S(1)}, f32[128]{0:T(128)}, u32[]{:S(2)}) copy-start(f32[128]{0:T(128)} %param.12) | copy-start | bytes 1540
  135.4 1.6 copy-start.18
  135.8 1.6 copy-start.5
  135.8 0.8 copy-start.16
  137.3 4.6 collective-permute-start
  141.9 21.5 %collective-permute-start.1 = (bf16[2,512,4,128]{3,1,2,0:T(8,128)(2,1)}, bf16[2,512,4,128]{3,1,2,0:T(8,128)(2,1)S(1)}, u32[]{:S(2)}, u32[]{:S(2)}) collective-permute-start(bf16[2,512,4,128]{3,1,2,0:T(8,128)(2,1)} %collective-permute-done), channel_id=1, source_target_pairs={{0,2},{2,4},{4,6},{6,8},{8,10},{10,12},{12,14},{14,16},{16,18},{18... | collective-permute-start | bytes 3145736 | tf_op jit(solution)/shard_map/ppermute | solution.py:18
  248.4 1.4 copy-start.20
  251.5 2.3 copy-start.7
  251.5 2.4 copy-start.15
  252.3 13.1 %copy-start.8 = (bf16[512,8,128]{2,0,1:T(8,128)(2,1)}, bf16[512,8,128]{2,0,1:T(8,128)(2,1)S(1)}, u32[]{:S(2)}) copy-start(bf16[512,8,128]{2,0,1:T(8,128)(2,1)S(1)} %copy.112) | copy-start | bytes 3145732
  265.3 11.7 %copy-start.12 = (bf16[512,1024]{0,1:T(8,128)(2,1)S(1)}, bf16[512,1024]{0,1:T(8,128)(2,1)}, u32[]{:S(2)}) copy-start(bf16[512,1024]{0,1:T(8,128)(2,1)} %copy.115) | copy-start | bytes 3145732
  277.0 12.6 %copy-start.10 = (bf16[4,128,2,512]{3,1,2,0:T(8,128)(2,1)}, bf16[4,128,2,512]{3,1,2,0:T(8,128)(2,1)S(1)}, u32[]{:S(2)}) copy-start(bf16[4,128,2,512]{3,1,2,0:T(8,128)(2,1)S(1)} %fusion.22) | copy-start | bytes 3145732
  305.6 8.6 %copy-start.1 = (bf16[4,2,512,1536]{2,3,1,0:T(8,128)(2,1)S(1)}, bf16[4,2,512,1536]{2,3,1,0:T(8,128)(2,1)}, u32[]{:S(2)}) copy-start(bf16[4,2,512,1536]{2,3,1,0:T(8,128)(2,1)} %fusion.1) | copy-start | bytes 37748740
  305.6 8.8 %copy-start.9 = (bf16[512,8,128]{2,0,1:T(8,128)(2,1)S(1)}, bf16[512,8,128]{2,0,1:T(8,128)(2,1)}, u32[]{:S(2)}) copy-start(bf16[512,8,128]{2,0,1:T(8,128)(2,1)} %copy-done.8) | copy-start | bytes 3145732
  327.1 15.3 %collective-permute-start.2 = (bf16[2,512,4,128]{3,1,2,0:T(8,128)(2,1)}, bf16[2,512,4,128]{3,1,2,0:T(8,128)(2,1)}, u32[]{:S(2)}, u32[]{:S(2)}) collective-permute-start(bf16[2,512,4,128]{3,1,2,0:T(8,128)(2,1)} %fusion.20), channel_id=1, source_target_pairs={{2,0},{4,2},{6,4},{8,6},{10,8},{12,10},{14,12},{16,14},{18,16},{20... | collective-permute-start | bytes 3145736 | tf_op jit(solution)/shard_map/ppermute | solution.py:18
  334.3 1.4 copy-start.3
  334.3 2.0 copy-start.4
  337.7 4.7 copy-start
  337.7 4.7 copy-start.2
  342.4 3.2 copy-start.13
  344.3 14.2 %collective-permute-start.3 = (bf16[2,512,4,128]{3,1,2,0:T(8,128)(2,1)S(1)}, bf16[2,512,4,128]{3,1,2,0:T(8,128)(2,1)S(1)}, u32[]{:S(2)}, u32[]{:S(2)}) collective-permute-start(bf16[2,512,4,128]{3,1,2,0:T(8,128)(2,1)S(1)} %fusion.18), channel_id=1, source_target_pairs={{2,0},{4,2},{6,4},{8,6},{10,8},{12,10},{14,12},{16,14},{18,16},{20... | collective-permute-start | bytes 3145736 | tf_op jit(solution)/shard_map/ppermute | solution.py:18
  359.6 1.8 copy-start.6
  359.6 1.8 copy-start.22
  361.0 1.1 copy-start.19
  361.0 1.2 copy-start.17
  393.3 198.2 %reduce-scatter.14.cloned.1.call-start = ((), (), s32[]{:S(2)}) async-start(), calls=%async_computation.8 | async-start | bytes 11698176
  419.8 1.3 copy-start.14
  419.8 298.8 %reduce-scatter.12.cloned.1.call-start = ((), (), s32[]{:S(2)}) async-start(), calls=%async_computation.7 | async-start | bytes 11698176
  447.2 1.2 copy-start.11
Sparse Core Ops, SparseCore 0:
  10.3 60.0 all-gather.5
  72.7 55.9 all-gather.3
  131.0 107.1 all-gather.7
  393.4 70.8 reduce-scatter.9
  468.8 122.6 reduce-scatter.13
  596.1 122.4 reduce-scatter.11
where the time goes:
time: 733 us; the launch traced here: 726 us
  waiting for transfers between devices  448 us (61%)
  matrix products  145 us (20%)
  local copies, waits for them, and re-layouts  68.2 us (9%)
  other arithmetic  25.8 us (4%)
  starting transfers between devices  23.3 us (3%)
  between operations  14.9 us (2%)
    unnamed x9, waiting for transfers between devices  265 us
    all_gather x1, waiting for transfers between devices, shards(): lax.all_gather(query_weight, 'ctx', axis=0, tiled=True)  71.6 us
    unnamed x55, local copies, waits for them, and re-layouts  61.1 us
    all_gather x1, waiting for transfers between devices, shards(): lax.all_gather(value_matrix, 'ctx', axis=0, tiled=True)  60 us
    all_gather x1, waiting for transfers between devices, shards(): lax.all_gather(key_matrix, 'ctx', axis=0, tiled=True)  50.8 us
    dot_general x3, matrix products, transposed(): lax.dot_general(left_rows, right_rows, (((1,), (1,)), ((), ())), preferre...  34.5 us
    ppermute x4, starting transfers between devices, passed_along(): return lax.ppermute(shard, axis, pairs)  23 us
    dot_general x2, matrix products, reduce_rows(): lax.dot_general(tokens, grad_rows, (((0,), (0,)), ((), ())), preferred_el...  23 us
  transfers between devices with their start and end apart: 10, of which 7 were waited for; matrix products, arithmetic and copies ran while one was open for 15% of the time, Pallas kernels for 0%

commit v1 on v0

--- a/solution.py
+++ b/solution.py
@@ -1,6 +1,10 @@
+import functools
+
 import jax
 import jax.numpy as jnp
 from jax import lax
+from jax.experimental import pallas as pl
+from jax.experimental.pallas import tpu as pltpu
 from jax.sharding import PartitionSpec as P
 
 HEAD_WIDTH = 128
@@ -10,6 +14,221 @@
 
 rope_base = 10000.0
 norm_eps = 1e-06
+
+
+MESH = pl.DeviceIdType.MESH
+
+
+def ring_place(size):
+    chips = size // 2
+    depth = chips // 2
+    me = lax.axis_index("ctx")
+    core = lax.rem(me, 2)
+    chip = lax.div(me, 2)
+    z, y = lax.div(chip, 2), lax.rem(chip, 2)
+    place = z + y * (2 * depth - 1 - 2 * z)
+
+    def at(offset, other=False):
+        spot = lax.rem(place + offset + chips, chips)
+        turned = lax.div(spot, depth)
+        row = spot + turned * (2 * depth - 1 - 2 * spot)
+        return (row * 2 + turned) * 2 + (1 - core if other else core)
+
+    return me, chips, at
+
+
+def meet(devices):
+    barrier = pltpu.get_barrier_semaphore()
+    for device in devices:
+        pl.semaphore_signal(barrier, inc=1, device_id={"ctx": device}, device_id_type=MESH)
+    pl.semaphore_wait(barrier, len(devices))
+
+
+def ring_streams(chips):
+    far = chips // 2
+    return ((0, 1, far), (0, -1, far - 1), (1, -1, far), (1, 1, far - 1))
+
+
+def gather_kernel(
+    size, shard_ref, whole_ref, own_sem, own_send, own_recv, send_sem, recv_sem, side_send, side_recv
+):
+    me, chips, at = ring_place(size)
+    half = shard_ref.shape[1] // 2
+    sibling = at(0, True)
+    streams = ring_streams(chips)
+    meet((at(1), at(-1), sibling))
+
+    def part(owner, which):
+        return whole_ref.at[owner, :, pl.ds(which * half, half)]
+
+    def send(src, dst, one, two, device):
+        copy = pltpu.make_async_remote_copy(
+            src_ref=src, dst_ref=dst, send_sem=one, recv_sem=two,
+            device_id={"ctx": device}, device_id_type=MESH,
+        )
+        copy.start()
+        return copy
+
+    started = {}
+    for k, (which, way, hops) in enumerate(streams):
+        started[k, 0] = send(
+            shard_ref.at[:, pl.ds(which * half, half)], part(me, which),
+            send_sem.at[k, 0], recv_sem.at[k, 0], at(way),
+        )
+    aside = [send(shard_ref, whole_ref.at[me], own_send, own_recv, sibling)]
+    mine = pltpu.make_async_copy(shard_ref, whole_ref.at[me], own_sem)
+    mine.start()
+    for step in range(chips // 2):
+        for k, (which, way, hops) in enumerate(streams):
+            if step >= hops:
+                continue
+            started[k, step].wait_recv()
+            block = part(at(-way * (step + 1)), which)
+            if step + 1 < hops:
+                started[k, step + 1] = send(
+                    block, block, send_sem.at[k, step + 1], recv_sem.at[k, step + 1], at(way)
+                )
+            aside.append(send(block, block, side_send.at[k, step], side_recv.at[k, step], sibling))
+    mine.wait()
+    for copy in started.values():
+        copy.wait_send()
+    for copy in aside:
+        copy.wait()
+
+
+def ring_gather(shard, collective_id):
+    size = lax.axis_size("ctx")
+    far = size // 4
+    dma = pltpu.SemaphoreType.DMA
+    return pl.pallas_call(
+        functools.partial(gather_kernel, size),
+        out_shape=jax.ShapeDtypeStruct((size,) + shard.shape, shard.dtype),
+        in_specs=[pl.BlockSpec(memory_space=pl.ANY)],
+        out_specs=pl.BlockSpec(memory_space=pl.ANY),
+        scratch_shapes=[dma, dma, dma] + [dma((4, far))] * 4,
+        compiler_params=pltpu.CompilerParams(collective_id=collective_id, has_side_effects=True),
+        cost_estimate=pl.CostEstimate(
+            flops=0, bytes_accessed=8 * size * shard.size * 2, transcendentals=0
+        ),
+    )(shard)
+
+
+def scatter_kernel(
+    size, turned_ref, back_ref, out_ref, own, mailed, arrived, passing,
+    side_send, side_recv, send_sem, recv_sem,
+):
+    me, chips, at = ring_place(size)
+    half = out_ref.shape[1] // 2
+    far = chips // 2
+    sibling = at(0, True)
+    streams = ring_streams(chips)
+    order = [far]
+    for distance in range(far - 1, 0, -1):
+        order += [distance, -distance]
+    order += [0]
+    slot_of = {offset: slot for slot, offset in enumerate(order)}
+    slot_of[-far] = slot_of[far]
+    meet((at(1), at(-1), sibling))
+
+    def term(owner, target, slot):
+        for which in range(2):
+            target[slot, which] = jnp.dot(
+                turned_ref[owner],
+                back_ref[:, which * half : (which + 1) * half],
+                preferred_element_type=jnp.float32,
+            ).astype(jnp.bfloat16)
+
+    sides = []
+
+    def compute(offset):
+        slot = slot_of[offset]
+        term(at(offset, True), mailed, slot)
+        copy = pltpu.make_async_remote_copy(
+            src_ref=mailed.at[slot], dst_ref=arrived.at[slot],
+            send_sem=side_send.at[slot], recv_sem=side_recv.at[slot],
+            device_id={"ctx": sibling}, device_id_type=MESH,
+        )
+        copy.start()
+        sides.append(copy)
+        term(at(offset), own, slot)
+
+    landed = set()
+
+    def pair_sum(offset, which):
+        slot = slot_of[offset]
+        if slot not in landed:
+            sides[slot].wait_recv()
+            landed.add(slot)
+        return own[slot, which].astype(jnp.float32) + arrived[slot, which].astype(jnp.float32)
+
+    started = {}
+    done = 0
+    for step in range(far):
+        needed = 1 + 2 * min(step + 1, far - 1)
+        while done < needed:
+            compute(order[done])
+            done += 1
+        for k, (which, way, hops) in enumerate(streams):
+            if step >= hops:
+                continue
+            offset = way * (hops - step)
+            total = pair_sum(offset, which)
+            if step:
+                started[k, step - 1].wait_recv()
+                source = passing.at[k, step - 1]
+                total = total + source[...].astype(jnp.float32)
+            else:
+                source = own.at[slot_of[offset], which]
+            source[...] = total.astype(jnp.bfloat16)
+            copy = pltpu.make_async_remote_copy(
+                src_ref=source, dst_ref=passing.at[k, step],
+                send_sem=send_sem.at[k, step], recv_sem=recv_sem.at[k, step],
+                device_id={"ctx": at(way)}, device_id_type=MESH,
+            )
+            copy.start()
+            started[k, step] = copy
+    while done < chips:
+        compute(order[done])
+        done += 1
+    for which in range(2):
+        total = pair_sum(0, which)
+        for k, (column, way, hops) in enumerate(streams):
+            if column == which:
+                started[k, hops - 1].wait_recv()
+                total = total + passing[k, hops - 1].astype(jnp.float32)
+        out_ref[:, which * half : (which + 1) * half] = total.astype(jnp.bfloat16)
+    for copy in sides:
+        copy.wait_send()
+    for copy in started.values():
+        copy.wait_send()
+
+
+def weight_gradient(turned, back, collective_id):
+    size = lax.axis_size("ctx")
+    chips = size // 2
+    far = chips // 2
+    rows, columns = turned.shape[1], back.shape[1]
+    half = columns // 2
+    dma = pltpu.SemaphoreType.DMA
+    vmem = pl.BlockSpec(memory_space=pltpu.VMEM)
+    block = (2, rows, half)
+    return pl.pallas_call(
+        functools.partial(scatter_kernel, size),
+        out_shape=jax.ShapeDtypeStruct((rows, columns), jnp.bfloat16),
+        in_specs=[vmem, vmem],
+        out_specs=vmem,
+        scratch_shapes=[pltpu.VMEM((chips,) + block, jnp.bfloat16)] * 3
+        + [pltpu.VMEM((4, far, rows, half), jnp.bfloat16)]
+        + [dma((chips,))] * 2
+        + [dma((4, far))] * 2,
+        compiler_params=pltpu.CompilerParams(
+            collective_id=collective_id, has_side_effects=True, vmem_limit_bytes=56 * 2**20
+        ),
+        cost_estimate=pl.CostEstimate(
+            flops=2 * turned.size * columns, bytes_accessed=8 * size * rows * columns * 2,
+            transcendentals=0,
+        ),
+    )(turned, back)
 
 
 def passed_along(shard, axis, by):
@@ -98,14 +317,14 @@
     score_scale = QUERY_SCALAR ** (-0.5)
     first_row = lax.axis_index("ctx") * row_count
     token_positions = (first_row + jnp.arange(row_count, dtype=jnp.int32)).astype(jnp.float32)
-    full_query, full_key, full_value = (
-        lax.all_gather(query_weight, "ctx", axis=0, tiled=True),
-        lax.all_gather(key_matrix, "ctx", axis=0, tiled=True),
-        lax.all_gather(value_matrix, "ctx", axis=0, tiled=True),
-    )
-    query_raw = jnp.dot(tokens, full_query, preferred_element_type=jnp.float32)
-    key_raw = jnp.dot(tokens, full_key, preferred_element_type=jnp.float32)
-    value_unprojected = jnp.dot(tokens, full_value, preferred_element_type=jnp.float32)
+    key_columns = key_matrix.shape[1]
+    width = tokens.shape[1]
+    size = lax.axis_size("ctx")
+    full_pair = ring_gather(jnp.concatenate([key_matrix, value_matrix], axis=1), 1)
+    flat_pair = full_pair.reshape(width, 2 * key_columns)
+    pair_raw = jnp.dot(tokens, flat_pair, preferred_element_type=jnp.float32)
+    key_raw, value_unprojected = pair_raw[:, :key_columns], pair_raw[:, key_columns:]
+    turned_tokens = tokens.T.reshape(size, width // size, row_count)
 
     def rotate_queries(unnormed_rows):
         return normalize_and_rotate(
@@ -117,22 +336,22 @@
             unnormed_rows, key_norm_gain, token_positions, heads_key, HEAD_WIDTH
         )
 
-    query_after_rotation, query_pull = jax.vjp(rotate_queries, query_raw)
     key_after_rotation, key_pullback = jax.vjp(rotate_keys, key_raw)
-    query_rows = query_after_rotation.astype(jnp.bfloat16).reshape(
-        row_count, heads_key, group_width, HEAD_WIDTH
-    )
     stacked = jnp.stack(
         [
             key_after_rotation.astype(jnp.bfloat16).reshape(row_count, heads_key, HEAD_WIDTH),
             value_unprojected.astype(jnp.bfloat16).reshape(row_count, heads_key, HEAD_WIDTH),
         ]
     )
-    arrivals = []
-    carried = stacked
-    for hop_count in range(reach_back):
-        carried = passed_along(carried, "ctx", 1)
-        arrivals.append(carried)
+    arrivals = [passed_along(stacked, "ctx", by) for by in range(1, reach_back + 1)]
+    query_weight, stacked = lax.optimization_barrier((query_weight, stacked))
+    full_query = ring_gather(query_weight, 2)
+    flat_query = full_query.reshape(width, query_weight.shape[1])
+    query_raw = jnp.dot(tokens, flat_query, preferred_element_type=jnp.float32)
+    query_after_rotation, query_pull = jax.vjp(rotate_queries, query_raw)
+    query_rows = query_after_rotation.astype(jnp.bfloat16).reshape(
+        row_count, heads_key, group_width, HEAD_WIDTH
+    )
     band_rows = jnp.concatenate(arrivals[::-1] + [stacked], axis=1)
     output_rows = cotangent.reshape(row_count, heads_key, group_width, HEAD_WIDTH)
     attended, query_grads, key_grads, value_grads = band_attention(
@@ -150,38 +369,46 @@
         lowest = (reach_back - distance) * row_count
         return band_grads[:, lowest : lowest + row_count]
 
-    returned = band_tile(reach_back)
-    for hop_count in range(1, reach_back + 1):
-        returned = passed_along(returned.astype(jnp.bfloat16), "ctx", -1).astype(
-            returned.dtype
-        ) + band_tile(reach_back - hop_count)
     (query_back,) = query_pull(query_grads.reshape(row_count, heads_query * HEAD_WIDTH))
+    query_back = query_back.astype(jnp.bfloat16)
+    returned = band_tile(0)
+    for by in range(1, reach_back + 1):
+        returned = returned + passed_along(
+            band_tile(by).astype(jnp.bfloat16), "ctx", -by
+        ).astype(jnp.float32)
+    query_gradient = weight_gradient(turned_tokens, query_back, 3)
     (key_backprop,) = key_pullback(returned[0].reshape(row_count, heads_key * HEAD_WIDTH))
-    query_back = query_back.astype(jnp.bfloat16)
     key_backprop = key_backprop.astype(jnp.bfloat16)
     value_backprop = returned[1].reshape(row_count, heads_key * HEAD_WIDTH).astype(jnp.bfloat16)
-    token_terms = (
-        transposed(query_back, full_query)
-        + transposed(key_backprop, full_key)
-        + transposed(value_backprop, full_value)
-    )
-    token_gradient = lax.psum_scatter(
-        token_terms.astype(jnp.bfloat16), "tp", scatter_dimension=1, tiled=True
-    )
-
-    def reduce_rows(grad_rows):
-        return lax.psum_scatter(
-            lax.dot_general(
-                tokens, grad_rows, (((0,), (0,)), ((), ())), preferred_element_type=jnp.float32
-            ).astype(jnp.bfloat16),
-            "ctx",
-            scatter_dimension=0,
-            tiled=True,
-        )
-
-    query_gradient = reduce_rows(query_back)
-    pair_gradient = reduce_rows(jnp.concatenate([key_backprop, value_backprop], axis=1))
-    key_columns = key_matrix.shape[1]
+    pair_back = jnp.concatenate([key_backprop, value_backprop], axis=1)
+    pair_back, query_gradient = lax.optimization_barrier((pair_back, query_gradient))
+
+    def token_terms(query_part, pair_part):
+        return (transposed(query_back, query_part) + transposed(pair_back, pair_part)).astype(
+            jnp.bfloat16
+        )
+
+    if lax.axis_size("tp") == 2:
+        group = lax.axis_index("tp")
+        query_halves = flat_query.reshape(2, width // 2, -1)
+        pair_halves = flat_pair.reshape(2, width // 2, -1)
+
+        def half_terms(which):
+            return token_terms(
+                lax.dynamic_index_in_dim(query_halves, which, 0, False),
+                lax.dynamic_index_in_dim(pair_halves, which, 0, False),
+            )
+
+        given = lax.ppermute(half_terms(1 - group), "tp", [(0, 1), (1, 0)])
+        pair_gradient = weight_gradient(turned_tokens, pair_back, 4)
+        token_gradient = (
+            half_terms(group).astype(jnp.float32) + given.astype(jnp.float32)
+        ).astype(jnp.bfloat16)
+    else:
+        token_gradient = lax.psum_scatter(
+            token_terms(flat_query, flat_pair), "tp", scatter_dimension=1, tiled=True
+        )
+        pair_gradient = weight_gradient(turned_tokens, pair_back, 4)
     return (
         attended.reshape(row_count, heads_query * HEAD_WIDTH),
         token_gradient,

time: 733 us -> 467 us (0.64)
  waiting for transfers between devices: 448 us -> 0.01 us
  Pallas kernels: 0 us -> 302 us
  matrix products: 145 us -> 103 us
  local copies, waits for them, and re-layouts: 68.2 us -> 29.6 us
  between operations: 14.9 us -> 1.7 us
  starting transfers between devices: 23.3 us -> 10.5 us
  other arithmetic: 25.8 us -> 15.1 us
    pallas_call x0 -> x4, Pallas kernels: none -> 302 us  [the longest x2 157 us: weight_gradient(): pl.pallas_call(functools.partial(scatter_kernel, size), out_shape=jax.Sha...]
    unnamed x9 -> x0, waiting for transfers between devices: 265 us -> none
    all_gather x3 -> x0, waiting for transfers between devices: 182 us -> none  [the longest x1 71.6 us: shards(): lax.all_gather(query_weight, 'ctx', axis=0, tiled=True)]
    unnamed x55 -> x82, local copies, waits for them, and re-layouts: 61.1 us -> 12.9 us
    dot_general x5 -> x2, matrix products: 47.2 us -> 20.7 us  [the longest x1 10.4 us: shards(): query_raw = jnp.dot(tokens, flat_query, preferred_element_type=jnp.float32)]
    dot_general x3 -> x4, matrix products: 34.5 us -> 20.4 us  [transposed(): lax.dot_general(left_rows, right_rows, (((1,), (1,)), ((), ())), preferre...]
    ppermute x4, starting transfers between devices: 23 us -> 9.06 us  [passed_along(): return lax.ppermute(shard, axis, pairs)]
    transpose x0 -> x1, local copies, waits for them, and re-layouts: none -> 8.48 us  [shards(): turned_tokens = tokens.T.reshape(size, width // size, row_count)]
  transfers between devices with their start and end apart: 10 -> 5, of which waited for: 7 -> 0; matrix products, arithmetic and copies ran while one was open for 15% -> 9% of each run, Pallas kernels for 0% -> 52%
where the time goes in v1:
time: 467 us; the launch traced here: 462 us
  Pallas kernels  302 us (65%)
  matrix products  103 us (22%)
  local copies, waits for them, and re-layouts  29.6 us (6%)
  other arithmetic  15.1 us (3%)
  starting transfers between devices  10.5 us (2%)
    pallas_call x2, Pallas kernels, weight_gradient(): pl.pallas_call(functools.partial(scatter_kernel, size), out_shape=jax.Sha...  157 us
    pallas_call x2, Pallas kernels, ring_gather(): pl.pallas_call(functools.partial(gather_kernel, size), out_shape=jax.Shap...  145 us
    dot_general x4, matrix products, transposed(): lax.dot_general(left_rows, right_rows, (((1,), (1,)), ((), ())), preferre...  20.4 us
    dot_general x1, matrix products, band_attention(): jnp.einsum('tkgd,ckd->kgtc', output_rows, value_row_block, preferred_elem...  15.8 us
    unnamed x82, local copies, waits for them, and re-layouts  12.9 us
    dot_general x1, matrix products, band_attention(): jnp.einsum('kgtc,tkgd->ckd', weights, output_rows, preferred_element_type...  12.4 us
    dot_general x1, matrix products, band_attention(): jnp.einsum('kgtc,ckd->tkgd', weights, value_row_block, preferred_element_...  11.6 us
    dot_general x1, matrix products, band_attention(): jnp.einsum('tkgd,ckd->kgtc', query_rows, key_row_block, preferred_element...  11.4 us
  transfers between devices with their start and end apart: 5, of which 0 were waited for; matrix products, arithmetic and copies ran while one was open for 9% of the time, Pallas kernels for 52%

profile of v1, /device:TPU:0, one launch (start us, length us, event | category | flops | bytes accessed | tf_op | source)
XLA Modules:
  0.0 461.9 jit_solution(11956153491497502786)
XLA Ops:
  0.6 2.0 pad_maximum_fusion.4.shard_ref
  2.6 60.9 %shard_map.110 = bf16[16,336,1024]{2,1,0:T(8,128)(2,1)} custom-call(bf16[336,1024]{1,0:T(8,128)(2,1)} %pad_maximum_fusion.4.shard_ref), custom_call_target="tpu_custom_call" | custom-call | bytes 88080384 | tf_op jit(solution)/shard_map/pallas_call | solution.py:103
  63.5 10.3 %convolution_bitcast_fusion.1 = f32[512,1024]{0,1:T(8,128)S(1)} fusion(bf16[5376,1024]{1,0:T(8,128)(2,1)} %bitcast.139, bf16[512,5376]{1,0:T(8,128)(2,1)} %param.7), kind=kOutput, calls=%fused_computation.45 | convolution fusion | flops 5637144576 | bytes 18612224 | tf_op jit(solution)/shard_map/dot_general | solution.py:325
  74.6 0.5 multiply_cosine_fusion
  75.4 1.0 copy.63
  76.8 0.4 fusion.41
  77.8 3.4 collective-permute-start
  81.1 3.1 collective-permute-start.1
  84.3 83.9 %shard_map.111 = bf16[16,336,1024]{2,1,0:T(8,128)(2,1)} custom-call(bf16[336,1024]{1,0:T(8,128)(2,1)} %shard_ref), custom_call_target="tpu_custom_call" | custom-call | bytes 88080384 | tf_op jit(solution)/shard_map/pallas_call | solution.py:103
  168.1 10.4 %multiply_reduce_fusion.2 = (f32[512,8]{0,1:T(8,128)S(1)}, f32[1024,512]{1,0:T(8,128)S(1)}) fusion(bf16[5376,1024]{1,0:T(8,128)(2,1)} %bitcast.144, bf16[512,5376]{1,0:T(8,128)(2,1)} %param.7), kind=kOutput, calls=%fused_computation.43 | convolution fusion | flops 5638189056 | bytes 18628608 | tf_op jit(solution)/shard_map/dot_general | solution.py:350
  178.6 2.0 multiply_multiply_fusion
  180.5 2.3 copy.67
  182.9 8.5 %copy.81 = bf16[5376,512]{1,0:T(8,128)(2,1)} copy(bf16[5376,512]{0,1:T(8,128)(2,1)} %bitcast.152) | data formatting | bytes 11010048 | tf_op jit(solution)/shard_map/transpose | solution.py:327
  191.3 0.3 subtract_convert_fusion
  191.8 1.2 compare_and_fusion
  193.0 1.3 constant_dynamic-update-slice_fusion.2
  194.3 1.4 constant_dynamic-update-slice_fusion.1
  195.8 11.4 %fusion.3 = (f32[4,2,512]{2,1,0:T(2,128)S(1)}, f32[4,1536,512,2]{2,1,3,0:T(8,128)}) fusion(pred[512,1536]{0,1:T(8,128)(4,1)S(1)} %compare_and_fusion, bf16[512,4,2,128]{0,3,2,1:T(8,128)(2,1)S(1)} %bitcast.155, bf16[2,1536,4,128]{3,1,2,0:T(8,128)(2,1)S(1)} %constant_dynamic-update-slice_fusion), kind=kOutput, calls=%fused_computation.5 | convolution fusion | flops 1629483008 | bytes 28590080 | tf_op jit(solution)/shard_map/tkgd,ckd->kgtc/dot_general | solution.py:264
  207.3 11.6 %fusion.36 = bf16[4,128,2,512]{3,1,2,0:T(8,128)(2,1)S(1)} fusion(bf16[2,1536,4,128]{3,1,2,0:T(8,128)(2,1)S(1)} %constant_dynamic-update-slice_fusion, f32[4,1536,512,2]{2,1,3,0:T(8,128)} %get-tuple-element.45, f32[4,2,512]{2,1,0:T(2,128)S(1)} %get-tuple-element.44, pred[512,1536]{0,1:T(8,128)(4,1)S(1)} %compare_and_fusion), kind=kOutput, calls=%fused_computation.49 | convolution fusion | flops 1636302848 | bytes 28590080 | tf_op jit(solution)/shard_map/kgtc,ckd->tkgd/dot_general | solution.py:278
  219.2 12.4 %fusion.27 = f32[1,1536,4,128]{3,1,2,0:T(8,128)} fusion(bf16[512,4,2,128]{0,3,2,1:T(8,128)(2,1)S(1)} %bitcast.159, f32[4,1536,512,2]{2,1,3,0:T(8,128)} %get-tuple-element.45, f32[4,2,512]{2,1,0:T(2,128)S(1)} %get-tuple-element.44, pred[512,1536]{0,1:T(8,128)(4,1)S(1)} %compare_and_fusion), kind=kOutput, calls=%fused_computation.30 | convolution fusion | flops 1635778560 | bytes 30162944 | tf_op jit(solution)/shard_map/kgtc,tkgd->ckd/dot_general | solution.py:299
  231.7 15.8 %fusion.1 = bf16[4,2,512,1536]{2,3,1,0:T(8,128)(2,1)} fusion(bf16[512,4,2,128]{0,3,2,1:T(8,128)(2,1)S(1)} %bitcast.160, f32[4,2,512]{2,1,0:T(2,128)S(1)} %bitcast.168, bf16[2,1536,4,128]{3,1,2,0:T(8,128)(2,1)} %copy-done.18, f32[4,2,512]{2,1,0:T(2,128)S(1)} %get-tuple-element.44, f32[4,1536,512,2]{2,1,3,0:T(8,128)} %get-tuple-element.45, ...), kind=kOutput, calls=%fused_computation.2 | convolution fusion | flops 1648361472 | bytes 41189376 | tf_op jit(solution)/shard_map/tkgd,ckd->kgtc/dot_general | solution.py:287
  247.5 7.1 %convolution_multiply_fusion = f32[4,128,2,512]{3,1,2,0:T(8,128)S(1)} fusion(bf16[4,2,512,1536]{2,3,1,0:T(8,128)(2,1)} %fusion.1, bf16[2,1536,4,128]{3,1,2,0:T(8,128)(2,1)} %copy-done.18), kind=kOutput, calls=%fused_computation.44 | convolution fusion | flops 1611137024 | bytes 16252928 | tf_op jit(solution)/shard_map/kgtc,ckd->tkgd/dot_general | solution.py:292
  254.6 1.5 copy-done
  256.3 3.5 fusion.31
  260.2 1.6 copy-done.5
  261.8 0.6 fusion.4
  262.4 1.5 fusion.54
  263.9 1.3 collective-permute-start.2
  265.2 1.3 collective-permute-start.3
  266.5 0.6 multiply_reduce_fusion
  267.1 1.7 fusion.32
  268.8 2.4 copy.99.back_ref
  271.2 91.0 %shard_map.112 = bf16[336,1024]{1,0:T(8,128)(2,1)} custom-call(bf16[16,336,512]{2,1,0:T(8,128)(2,1)} %bitcast.153, bf16[512,1024]{1,0:T(8,128)(2,1)} %copy.99.back_ref), custom_call_target="tpu_custom_call" | custom-call | flops 5637144576 | bytes 88080384 | tf_op jit(solution)/shard_map/pallas_call | solution.py:215
  362.2 2.0 fusion.35
  364.4 1.5 copy-done.15
  366.0 0.4 multiply_add_fusion.1
  366.5 0.6 multiply_reduce_fusion.3
  367.2 1.0 copy_bitcast_fusion.1
  368.2 0.4 copy.80
  368.9 3.2 fusion.9
  372.4 4.7 %add_convert_fusion.1 = bf16[512,2688]{1,0:T(8,128)(2,1)} fusion(f32[512,2688]{1,0:T(8,128)S(1)} %fusion.9, bf16[512,1024]{0,1:T(8,128)(2,1)S(1)} %bitcast.163, bf16[2,2688,1024]{2,1,0:T(8,128)(2,1)S(1)} %bitcast.147, s32[]{:T(128)S(6)} %select_n.15), kind=kOutput, calls=%fused_computation.23 | convolution fusion | flops 2821324800 | bytes 14811140 | tf_op jit(solution)/shard_map/dot_general | solution.py:306
  377.0 1.5 collective-permute-start.4
  378.5 1.5 copy.82
  380.0 66.3 %shard_map.113 = bf16[336,1024]{1,0:T(8,128)(2,1)} custom-call(bf16[16,336,512]{2,1,0:T(8,128)(2,1)} %bitcast.154, bf16[512,1024]{1,0:T(8,128)(2,1)} %copy-done.20), custom_call_target="tpu_custom_call" | custom-call | flops 5637144576 | bytes 88080384 | tf_op jit(solution)/shard_map/pallas_call | solution.py:215
  446.3 2.0 fusion.55
  448.3 6.2 %fusion.13 = f32[512,2688]{1,0:T(8,128)S(1)} fusion(bf16[512,1024]{1,0:T(8,128)(2,1)} %copy-done.20, bf16[2,2688,1024]{2,1,0:T(8,128)(2,1)} %bitcast.140, s32[]{:T(128)S(6)} %select_n.14), kind=kOutput, calls=%fused_computation.18 | convolution fusion | flops 2818572288 | bytes 12058628 | tf_op jit(solution)/shard_map/dot_general | solution.py:306
  454.6 6.3 %add_convert_fusion = bf16[512,2688]{1,0:T(8,128)(2,1)} fusion(bf16[512,2688]{1,0:T(8,128)(2,1)} %collective-permute-done.4, f32[512,2688]{1,0:T(8,128)S(1)} %fusion.13, bf16[512,1024]{0,1:T(8,128)(2,1)S(1)} %bitcast.164, bf16[2,2688,1024]{2,1,0:T(8,128)(2,1)S(1)} %bitcast.150, s32[]{:T(128)S(6)} %select_n.14), kind=kOutput, calls=%fused_computation.22 | convolution fusion | flops 2826829824 | bytes 17563652 | tf_op jit(solution)/shard_map/dot_general | solution.py:306
  460.9 0.8 copy.112
  (106 shorter events, 3.7 us)
Async XLA Ops:
  74.0 2.5 copy-start.27
  74.1 2.7 copy-start.24
  74.5 2.7 copy-start.3
  74.6 1.9 copy-start.22
  75.3 2.0 copy-start.14
  75.4 1.8 copy-start.16
  76.4 1.0 copy-start.19
  77.8 115.2 %collective-permute-start = (bf16[2,512,4,128]{3,1,2,0:T(8,128)(2,1)S(1)}, bf16[2,512,4,128]{3,1,2,0:T(8,128)(2,1)}, u32[]{:S(2)}, u32[]{:S(2)}) collective-permute-start(bf16[2,512,4,128]{3,1,2,0:T(8,128)(2,1)S(1)} %pad_maximum_fusion.1), channel_id=1, source_target_pairs={{0,4},{2,6},{4,8},{6,10},{8,12},{10,14},{12,16},{14,18},{16,20},{1... | collective-permute-start | bytes 3145736 | tf_op jit(solution)/shard_map/ppermute | solution.py:237
  81.1 113.2 %collective-permute-start.1 = (bf16[2,512,4,128]{3,1,2,0:T(8,128)(2,1)S(1)}, bf16[2,512,4,128]{3,1,2,0:T(8,128)(2,1)}, u32[]{:S(2)}, u32[]{:S(2)}) collective-permute-start(bf16[2,512,4,128]{3,1,2,0:T(8,128)(2,1)S(1)} %pad_maximum_fusion.1), channel_id=1, source_target_pairs={{0,2},{2,4},{4,6},{6,8},{8,10},{10,12},{12,14},{14,16},{16,18},{18... | collective-permute-start | bytes 3145736 | tf_op jit(solution)/shard_map/ppermute | solution.py:237
  168.1 10.4 %copy-start.26 = (f32[128]{0:T(128)S(1)}, f32[128]{0:T(128)}, u32[]{:S(2)}) copy-start(f32[128]{0:T(128)} %param.11) | copy-start | bytes 1540
  178.5 4.3 copy-start.1
  182.9 8.5 %copy-start.7 = (f32[512,8,128]{0,2,1:T(8,128)S(1)}, f32[512,8,128]{0,2,1:T(8,128)}, u32[]{:S(2)}) copy-start(f32[512,8,128]{0,2,1:T(8,128)} %multiply_multiply_fusion) | copy-start | bytes 6291460
  191.8 4.1 copy-start.8
  195.8 11.4 %copy-start.18 = (bf16[2,1536,4,128]{3,1,2,0:T(8,128)(2,1)}, bf16[2,1536,4,128]{3,1,2,0:T(8,128)(2,1)S(1)}, u32[]{:S(2)}) copy-start(bf16[2,1536,4,128]{3,1,2,0:T(8,128)(2,1)S(1)} %constant_dynamic-update-slice_fusion) | copy-start | bytes 9437188
  207.2 11.7 %copy-start.12 = (bf16[512,1024]{0,1:T(8,128)(2,1)S(1)}, bf16[512,1024]{0,1:T(8,128)(2,1)}, u32[]{:S(2)}) copy-start(bf16[512,1024]{0,1:T(8,128)(2,1)} %copy.67) | copy-start | bytes 3145732
  218.9 12.8 %copy-start.10 = (bf16[4,128,2,512]{3,1,2,0:T(8,128)(2,1)}, bf16[4,128,2,512]{3,1,2,0:T(8,128)(2,1)S(1)}, u32[]{:S(2)}) copy-start(bf16[4,128,2,512]{3,1,2,0:T(8,128)(2,1)S(1)} %fusion.36) | copy-start | bytes 3145732
  247.5 8.6 %copy-start = (bf16[4,2,512,1536]{2,3,1,0:T(8,128)(2,1)S(1)}, bf16[4,2,512,1536]{2,3,1,0:T(8,128)(2,1)}, u32[]{:S(2)}) copy-start(bf16[4,2,512,1536]{2,3,1,0:T(8,128)(2,1)} %fusion.1) | copy-start | bytes 37748740
  247.5 8.9 %copy-start.9 = (bf16[512,8,128]{0,2,1:T(8,128)(2,1)S(1)}, bf16[512,8,128]{0,2,1:T(8,128)(2,1)}, u32[]{:S(2)}) copy-start(bf16[512,8,128]{0,2,1:T(8,128)(2,1)} %copy-done.8) | copy-start | bytes 3145732
  259.9 1.9 copy-start.5
  262.4 4.1 copy-start.2
  263.9 98.3 %collective-permute-start.2 = (bf16[2,512,4,128]{3,1,2,0:T(8,128)(2,1)}, bf16[2,512,4,128]{3,1,2,0:T(8,128)(2,1)}, u32[]{:S(2)}, u32[]{:S(2)}) collective-permute-start(bf16[2,512,4,128]{3,1,2,0:T(8,128)(2,1)} %get-tuple-element.28), channel_id=1, source_target_pairs={{2,0},{4,2},{6,4},{8,6},{10,8},{12,10},{14,12},{16,14},{18,16},{20... | collective-permute-start | bytes 3145736 | tf_op jit(solution)/shard_map/ppermute | solution.py:237
  265.2 97.0 %collective-permute-start.3 = (bf16[2,512,4,128]{3,1,2,0:T(8,128)(2,1)}, bf16[2,512,4,128]{3,1,2,0:T(8,128)(2,1)}, u32[]{:S(2)}, u32[]{:S(2)}) collective-permute-start(bf16[2,512,4,128]{3,1,2,0:T(8,128)(2,1)} %get-tuple-element.29), channel_id=1, source_target_pairs={{4,0},{6,2},{8,4},{10,6},{12,8},{14,10},{16,12},{18,14},{20,16},{2... | collective-permute-start | bytes 3145736 | tf_op jit(solution)/shard_map/ppermute | solution.py:237
  271.2 91.0 %copy-start.6 = (f32[1,1536,4,128]{3,1,2,0:T(8,128)S(1)}, f32[1,1536,4,128]{3,1,2,0:T(8,128)}, u32[]{:S(2)}) copy-start(f32[1,1536,4,128]{3,1,2,0:T(8,128)} %fusion.27) | copy-start | bytes 9437188
  362.2 6.6 %slice-start = ((s8[11010048]{0:T(1024)(128)(4,1)}), s8[4194304]{0:T(1024)(128)(4,1)S(1)}, s32[]{:S(2)}) async-start(s8[11010048]{0:T(1024)(128)(4,1)} %bitcast.141), calls=%async_computation | async-start | bytes 8388608
  362.2 6.6 %slice-start.1 = ((s8[11010048]{0:T(1024)(128)(4,1)}), s8[4194304]{0:T(1024)(128)(4,1)S(1)}, s32[]{:S(2)}) async-start(s8[11010048]{0:T(1024)(128)(4,1)} %bitcast.141), calls=%async_computation.1 | async-start | bytes 8388608
  364.2 1.7 copy-start.15
  364.2 1.8 copy-start.17
  364.3 2.1 copy-start.4
  364.3 2.1 copy-start.28
  366.0 1.1 copy-start.25
  366.0 1.2 copy-start.23
  366.5 2.4 slice-start.2
  367.2 5.0 %slice-start.3 = ((s8[11010048]{0:T(1024)(128)(4,1)}), s8[4194304]{0:T(1024)(128)(4,1)S(1)}, s32[]{:S(2)}) async-start(s8[11010048]{0:T(1024)(128)(4,1)} %bitcast.145), calls=%async_computation.3 | async-start | bytes 8388608
  368.7 3.5 slice-start.4
  368.8 3.3 copy-start.20
  368.9 3.3 slice-start.5
  368.9 3.5 copy-start.13
  372.4 6.1 %copy-start.11 = (bf16[4,128,2,512]{3,1,2,0:T(8,128)(2,1)S(1)}, bf16[4,128,2,512]{3,1,2,0:T(8,128)(2,1)}, u32[]{:S(2)}) copy-start(bf16[4,128,2,512]{3,1,2,0:T(8,128)(2,1)} %copy-done.10) | copy-start | bytes 3145732
  377.0 77.5 %collective-permute-start.4 = (bf16[512,2688]{1,0:T(8,128)(2,1)}, bf16[512,2688]{1,0:T(8,128)(2,1)}, u32[]{:S(2)}, u32[]{:S(2)}) collective-permute-start(bf16[512,2688]{1,0:T(8,128)(2,1)} %add_convert_fusion.1), channel_id=1, source_target_pairs={{0,1},{1,0},{2,3},{3,2},{4,5},{5,4},{6,7},{7,6},{8,9},{9,8},{10,11... | collective-permute-start | bytes 8257544 | tf_op jit(solution)/shard_map/ppermute | solution.py:402
  380.0 74.5 %slice-start.6 = ((s8[11010048]{0:T(1024)(128)(4,1)}), s8[4194304]{0:T(1024)(128)(4,1)S(1)}, s32[]{:S(2)}) async-start(s8[11010048]{0:T(1024)(128)(4,1)} %bitcast.148), calls=%async_computation.6 | async-start | bytes 8388608
  380.0 74.5 %slice-start.7 = ((s8[11010048]{0:T(1024)(128)(4,1)}), s8[2621440]{0:T(1024)(128)(4,1)S(1)}, s32[]{:S(2)}) async-start(s8[11010048]{0:T(1024)(128)(4,1)} %bitcast.148), calls=%async_computation.7 | async-start | bytes 5242880
  448.3 6.3 %slice-start.8 = ((s8[11010048]{0:T(1024)(128)(4,1)}), s8[4194304]{0:T(1024)(128)(4,1)S(1)}, s32[]{:S(2)}) async-start(s8[11010048]{0:T(1024)(128)(4,1)} %bitcast.148), calls=%async_computation.8 | async-start | bytes 8388608
  454.5 6.4 %copy-start.21 = (bf16[336,1024]{1,0:T(8,128)(2,1)S(1)}, bf16[336,1024]{1,0:T(8,128)(2,1)}, u32[]{:S(2)}) copy-start(bf16[336,1024]{1,0:T(8,128)(2,1)} %shard_map.112) | copy-start | bytes 2064388
